TPU v7x, 128 devices: a whole 4x4x4 slice. The times are simulated.
128 devices in a mesh: group: 4 (over y), table: 32 (over x, z, core).
Axes of the slice: x: 4, y: 4, z: 4, core: 2. Of those that a mesh axis runs over, the one named last changes fastest.
Arguments:
- user_vec: bfloat16 [16384, 256], P(('group', 'table')), may hold values from -12 to 12
- cluster_rows: bfloat16 [65536, 256], P(('group', 'table')), may hold values from -0.5625 to 0.5625
- leaf_rows: bfloat16 [256, 4096, 256], P(('group', 'table')), may hold values from -0.5625 to 0.5625
- touched: int32 [256], P(('group', 'table')), may hold values from 0 to 511, as said below
- route_owner: int32 [16384], P(('group', 'table')), may hold values from 0 to 127, as said below
- route_slot: int32 [16384], P(('group', 'table')), may hold values from 0 to 1
- leaf_label: int32 [16384], P(('group', 'table')), may hold values from 0 to 4095
Outputs:
- user_grad: float32 [16384, 256], P(('group', 'table'))
- cluster_grad: float32 [65536, 256], P(('group', 'table'))
- leaf_grad: bfloat16 [256, 4096, 256], P(('group', 'table'))
Inputs may be any that keep to these rules, and one draw needn't show every extreme that they name: `touched`: the 2 entries of one owner are distinct local cluster indices. `route_owner`: among the 128 users of one device at most 2 name the same owner, and one owner is named by 2 users of every device.
All inputs are finite; a program needn't handle non-finite values.
Results may differ from a plain program's by a relative error of at most 0.0034.
Values may be sent and summed in bfloat16 or wider, within the bound.
No kernel may reach another device: no remote copies, remote signals or barrier semaphores. Data moves between devices by JAX's collectives and lax.ppermute only.
A program may use at most 192 MiB of HBM per device.

v0:
```python
import math

import jax
import jax.numpy as jnp
from jax import lax
from jax.sharding import PartitionSpec as P


def merged(x, axis, combine):
    everything = jax.tree.map(lambda part: lax.all_gather(part, axis), x)
    leading = jax.tree.map(lambda part: part[0], everything)

    def hop(k, so_far):
        return combine(so_far, jax.tree.map(lambda part: part[k], everything))

    return lax.fori_loop(1, lax.axis_size(axis), hop, leading)


def leaf_pass(recv_users, recv_meta, cluster_rows, leaf_rows, touched):
    slot_ids = recv_meta[:, 0]
    leaf_ids = recv_meta[:, 1]
    is_live = slot_ids >= 0
    local_ids = touched[jnp.maximum(slot_ids, 0)]
    leaf_count = leaf_rows.shape[1]
    targets = (leaf_ids[:, None] == jnp.arange(leaf_count)[None, :]).astype(jnp.float32)
    user_part = jnp.zeros(recv_users.shape, jnp.float32)
    table_parts = []
    for table_index in range(leaf_rows.shape[0]):
        leaf_table = leaf_rows[table_index]
        scores = lax.dot_general(
            recv_users, leaf_table, (((1,), (1,)), ((), ())), preferred_element_type=jnp.float32
        )
        peak = jnp.max(scores, axis=1, keepdims=True)
        weights = jnp.exp(scores - peak)
        weights = weights / jnp.sum(weights, axis=1, keepdims=True)
        chosen = (slot_ids == table_index).astype(jnp.float32)[:, None]
        coeffs = ((weights - targets) * chosen).astype(jnp.bfloat16)
        user_part = user_part + jnp.dot(coeffs, leaf_table, preferred_element_type=jnp.float32)
        table_parts.append(
            lax.dot_general(
                coeffs, recv_users, (((0,), (0,)), ((), ())), preferred_element_type=jnp.float32
            ).astype(jnp.bfloat16)
        )
    label_rows = cluster_rows[local_ids].astype(jnp.float32) * is_live[:, None].astype(jnp.float32)
    cluster_count = cluster_rows.shape[0]
    picks = ((local_ids[:, None] == jnp.arange(cluster_count)[None, :]) & is_live[:, None]).astype(
        jnp.bfloat16
    )
    label_sums = lax.dot_general(
        picks, recv_users, (((0,), (0,)), ((), ())), preferred_element_type=jnp.float32
    )
    return (user_part - label_rows, jnp.stack(table_parts), label_sums)


def combine_totals(earlier_part, later_part):
    peak = jnp.maximum(earlier_part[0], later_part[0])
    summed = earlier_part[1] * jnp.exp(earlier_part[0] - peak) + later_part[1] * jnp.exp(
        later_part[0] - peak
    )
    return (peak, summed)


def score_block(user_block, cluster_rows):
    return lax.dot_general(
        user_block, cluster_rows, (((1,), (1,)), ((), ())), preferred_element_type=jnp.float32
    )


def place_ranks(owner_ids):
    per_dev = owner_ids.shape[-1]
    matches = owner_ids[..., :, None] == owner_ids[..., None, :]
    before = jnp.arange(per_dev)[None, :] < jnp.arange(per_dev)[:, None]
    return jnp.sum((matches & before).astype(jnp.int32), axis=-1)


def per_device(user_vec, cluster_rows, leaf_rows, touched, route_owner, route_slot, leaf_label):
    owners_n = lax.axis_size(("group", "table"))
    per_dev = user_vec.shape[0]
    feature_width = user_vec.shape[1]
    slot_cap = max(2, 2 * per_dev // owners_n)
    capacity = owners_n * slot_cap
    gathered = lax.all_gather(user_vec, ("group", "table"), axis=0, tiled=True)
    position = route_owner * slot_cap + place_ranks(route_owner)
    send_users = jnp.zeros((capacity, feature_width), jnp.bfloat16).at[position].set(user_vec)
    send_meta = (
        jnp.full((capacity, 2), -1, jnp.int32)
        .at[position]
        .set(jnp.stack([route_slot, leaf_label], axis=1))
    )
    recv_users, recv_meta = (
        lax.all_to_all(
            send_users.reshape(owners_n, slot_cap, feature_width),
            ("group", "table"),
            split_axis=0,
            concat_axis=0,
            tiled=True,
        ),
        lax.all_to_all(
            send_meta.reshape(owners_n, slot_cap, 2),
            ("group", "table"),
            split_axis=0,
            concat_axis=0,
            tiled=True,
        ),
    )
    user_part, leaf_grad, label_sums = leaf_pass(
        recv_users.reshape(capacity, feature_width),
        recv_meta.reshape(capacity, 2),
        cluster_rows,
        leaf_rows,
        touched,
    )
    returned = lax.all_to_all(
        user_part.reshape(owners_n, slot_cap, feature_width),
        ("group", "table"),
        split_axis=0,
        concat_axis=0,
        tiled=True,
    )
    home_part = returned.reshape(capacity, feature_width)[position]
    user_total = gathered.shape[0]
    block_len = math.gcd(user_total, 2048)
    user_blocks = gathered.reshape(user_total // block_len, block_len, feature_width)

    def block_stats(user_block):
        scores = score_block(user_block, cluster_rows)
        peak = jnp.max(scores, axis=1)
        return (peak, jnp.sum(jnp.exp(scores - peak[:, None]), axis=1))

    peaks, sums = lax.map(block_stats, user_blocks)
    peak_all, total_exp = merged(
        (peaks.reshape(user_total), sums.reshape(user_total)), ("group", "table"), combine_totals
    )
    log_total = peak_all + jnp.log(total_exp)
    log_blocks = log_total.reshape(user_total // block_len, block_len)

    def add_cluster(carry, inputs):
        user_block, log_block = inputs
        probs_bf = jnp.exp(score_block(user_block, cluster_rows) - log_block[:, None]).astype(
            jnp.bfloat16
        )
        return (
            carry
            + lax.dot_general(
                probs_bf, user_block, (((0,), (0,)), ((), ())), preferred_element_type=jnp.float32
            ),
            None,
        )

    prob_sums = lax.scan(
        add_cluster, jnp.zeros(cluster_rows.shape, jnp.float32), (user_blocks, log_blocks)
    )[0]
    row_count = per_dev * lax.axis_size(("group", "table"))
    inner_len = math.gcd(row_count, 2048)
    part_users = gathered.reshape(row_count // inner_len, inner_len, feature_width)
    part_logs = log_total.reshape(row_count // inner_len, inner_len)

    def one_block(inputs):
        user_block, log_block = inputs
        probs_bf = jnp.exp(score_block(user_block, cluster_rows) - log_block[:, None]).astype(
            jnp.bfloat16
        )
        return jnp.dot(probs_bf, cluster_rows, preferred_element_type=jnp.float32)

    result = lax.map(one_block, (part_users, part_logs)).reshape(row_count, feature_width)
    user_grad = lax.psum_scatter(result, ("group", "table"), scatter_dimension=0, tiled=True)
    user_grad = user_grad + home_part
    return (user_grad, prob_sums - label_sums, leaf_grad)


def solution(mesh):
    in_specs = (
        P(("group", "table"), None),
        P(("group", "table"), None),
        P(("group", "table"), None, None),
        P(("group", "table")),
        P(("group", "table")),
        P(("group", "table")),
        P(("group", "table")),
    )
    out_specs = (
        P(("group", "table"), None),
        P(("group", "table"), None),
        P(("group", "table"), None, None),
    )
    return jax.shard_map(
        per_device, mesh=mesh, in_specs=in_specs, out_specs=out_specs, check_vma=False
    )
```

profile of v0, /device:TPU:0, one launch (start us, length us, event | category | flops | bytes accessed | tf_op | source)
XLA Modules:
  0.0 1141.9 jit_solution(5647131816446998337)
XLA Ops:
  8.0 75.6 %all-gather.6.cloned.1.call-done = bf16[16384,256]{1,0:T(8,128)(2,1)} async-done(((bf16[128,256]{1,0:T(8,128)(2,1)}), bf16[16384,256]{1,0:T(8,128)(2,1)}) %all-gather.6.cloned.1.call-update) | async-done | bytes 8388624 | tf_op jit(solution)/shard_map/all_gather | solution.py:82
  83.6 24.8 %while.50 = (s32[]{:T(128)}, f32[8,2048]{1,0:T(8,128)S(1)}, f32[8,2048]{1,0:T(8,128)S(1)}, bf16[8,2048,256]{2,1,0:T(8,128)(2,1)}, bf16[512,256]{1,0:T(8,128)(2,1)}, /*index=5*/s32[]{:T(128)}, s32[]{:T(128)}) while((s32[]{:T(128)}, f32[8,2048]{1,0:T(8,128)S(1)}, f32[8,2048]{1,0:T(8,128)S(1)}, bf16[8,2048,256]{2,1,0:T(8,128)(2,1)}, ...), condition=%wide.region_3.0_spmd, body=%wide.region_0.3_spmd.sunk | while | flops 540012544 | bytes 9757269 | solution.py:130
  83.6 2.0 fusion.82
  86.7 2.0 fusion.82
  89.8 2.0 fusion.82
  92.9 2.0 fusion.82
  96.0 2.0 fusion.82
  99.1 2.0 fusion.82
  102.2 2.0 fusion.82
  105.3 2.0 fusion.82
  110.0 67.0 %all-gather.10.cloned.1.call-done = f32[128,1,16384]{2,1,0:T(1,128)} async-done(((f32[1,1,16384]{2,1,0:T(1,128)}), f32[128,1,16384]{2,1,0:T(1,128)}) %all-gather.10.cloned.1.call-update) | async-done | bytes 8388624 | tf_op jit(solution)/shard_map/all_gather | solution.py:10
  177.0 13.1 %copy.24 = f32[128,1,16384]{2,0,1:T(8,128)} copy(f32[128,1,16384]{2,1,0:T(1,128)} %all-gather.10.cloned.1.call-done) | data formatting | bytes 16777216
  190.1 58.1 %all-gather.8.cloned.1.call-done = f32[128,1,16384]{2,1,0:T(1,128)} async-done(((f32[1,1,16384]{2,1,0:T(1,128)}), f32[128,1,16384]{2,1,0:T(1,128)}) %all-gather.8.cloned.1.call-update) | async-done | bytes 8388624 | tf_op jit(solution)/shard_map/all_gather | solution.py:10
  248.2 13.4 %copy.25 = f32[128,1,16384]{2,0,1:T(8,128)} copy(f32[128,1,16384]{2,1,0:T(1,128)} %all-gather.8.cloned.1.call-done) | data formatting | bytes 16777216
  261.6 176.6 %while.51 = (s32[]{:T(128)}, f32[16384]{0:T(1024)S(1)}, f32[16384]{0:T(1024)S(1)}, f32[128,16384]{1,0:T(8,128)}, f32[128,16384]{1,0:T(8,128)}, /*index=5*/s32[]{:T(128)}, s32[]{:T(128)}, s32[]{:T(128)}) while((s32[]{:T(128)}, f32[16384]{0:T(1024)S(1)}, f32[16384]{0:T(1024)S(1)}, f32[128,16384]{1,0:T(8,128)}, f32[128,16384]{1,0:T(8,128)}, ...), condition=%wide.region_5.0_spmd, body=%wide.region_4.0_spmd.sunk | while | flops 98309 | bytes 655491 | solution.py:16
  270.0 1.3 constant_dynamic-slice_fusion.7
  438.3 31.8 %while.52 = (s32[]{:T(128)}, f32[8,2048,256]{2,1,0:T(8,128)}, bf16[8,2048,256]{2,1,0:T(8,128)(2,1)}, bf16[512,256]{1,0:T(8,128)(2,1)S(1)}, f32[8,2048]{1,0:T(8,128)S(1)}, /*index=5*/s32[]{:T(128)}) while((s32[]{:T(128)}, f32[8,2048,256]{2,1,0:T(8,128)}, bf16[8,2048,256]{2,1,0:T(8,128)(2,1)}, bf16[512,256]{1,0:T(8,128)(2,1)S(1)}, ...), condition=%wide.region_7.8_spmd, body=%wide.region_6.0_spmd.sunk | while | flops 1075838976 | bytes 3695689 | solution.py:165
  438.3 4.0 fusion.86
  442.3 3.9 fusion.86
  446.2 4.0 fusion.86
  450.2 4.0 fusion.86
  454.2 4.0 fusion.86
  458.2 4.0 fusion.86
  462.2 3.9 fusion.86
  466.1 3.9 fusion.86
  471.9 1.5 copy.18
  473.5 6.2 all-to-all-start.1
  480.3 1.4 scatter_custom_fusion
  482.4 7.0 all-to-all-done.1
  489.4 4.6 all-to-all-start
  496.6 7.1 all-to-all-done
  503.8 2.6 fusion.56
  508.7 3.5 fusion.22
  515.1 4.6 all-to-all-start.2
  519.7 2.4 fusion.19
  522.8 2.4 pad_maximum_fusion
  525.2 6.3 all-to-all-done.2
  532.4 30.9 %while.53 = (s32[]{:T(128)}, f32[512,256]{1,0:T(8,128)S(1)}, bf16[8,2048,256]{2,1,0:T(8,128)(2,1)}, bf16[512,256]{1,0:T(8,128)(2,1)S(1)}, f32[8,2048]{1,0:T(8,128)S(1)}, /*index=5*/s32[]{:T(128)}, s32[]{:T(128)}) while((s32[]{:T(128)}, f32[512,256]{1,0:T(8,128)S(1)}, bf16[8,2048,256]{2,1,0:T(8,128)(2,1)}, ...), condition=%wide.region_17.18_spmd.clone, body=%wide.region_16.17_spmd.clone.sunk | while | flops 1076101120 | bytes 3433563 | solution.py:150
  532.5 3.8 fusion.90
  536.3 3.9 fusion.90
  540.3 3.8 fusion.90
  544.2 3.8 fusion.90
  548.0 3.8 fusion.90
  551.8 3.8 fusion.90
  555.6 3.8 fusion.90
  559.5 3.8 fusion.90
  564.6 569.2 %reduce-scatter.2.cloned.1.call-done = f32[128,256]{1,0:T(8,128)} async-done(((f32[16384,256]{1,0:T(8,128)}), f32[128,256]{1,0:T(8,128)}) %reduce-scatter.2.cloned.1.call-update) | async-done | bytes 131088 | tf_op jit(solution)/shard_map/reduce_scatter | solution.py:166
  1133.8 1.6 add.96
  (352 shorter events, 197.2 us)
Async XLA Ops:
  7.2 76.4 %all-gather.6.cloned.1.call-start = ((), (), s32[]{:S(2)}) async-start(), calls=%async_computation.4 | async-start | bytes 8454144 | tf_op jit(solution)/shard_map/all_gather | solution.py:82
  7.9 169.1 %all-gather.10.cloned.1.call-start = ((), (), s32[]{:S(2)}) async-start(), calls=%async_computation.7 | async-start | bytes 8454144 | tf_op jit(solution)/shard_map/all_gather | solution.py:10
  109.1 139.1 %all-gather.8.cloned.1.call-start = ((), (), s32[]{:S(2)}) async-start(), calls=%async_computation.6 | async-start | bytes 8454144 | tf_op jit(solution)/shard_map/all_gather | solution.py:10
  109.9 1023.8 %reduce-scatter.2.cloned.1.call-start = ((), (), s32[]{:S(2)}) async-start(), calls=%async_computation.5 | async-start | bytes 16908288 | tf_op jit(solution)/shard_map/reduce_scatter | solution.py:166
  190.1 71.5 %slice-start = ((f32[128,1,16384]{2,1,0:T(1,128)}), f32[1,1,16384]{2,1,0:T(1,128)S(1)}, s32[]{:S(2)}) async-start(f32[128,1,16384]{2,1,0:T(1,128)} %all-gather.10.cloned.1.call-done), calls=%async_computation.8 | async-start | bytes 131072 | tf_op jit(solution)/shard_map/slice | solution.py:11
  190.1 248.2 %copy-start = (bf16[512,256]{1,0:T(8,128)(2,1)S(1)}, bf16[512,256]{1,0:T(8,128)(2,1)}, u32[]{:S(2)}) copy-start(bf16[512,256]{1,0:T(8,128)(2,1)} %get-tuple-element.528) | copy-start | bytes 786436
  248.2 13.4 %slice-start.1 = ((f32[128,1,16384]{2,1,0:T(1,128)}), f32[1,1,16384]{2,1,0:T(1,128)S(1)}, s32[]{:S(2)}) async-start(f32[128,1,16384]{2,1,0:T(1,128)} %all-gather.8.cloned.1.call-done), calls=%async_computation.9 | async-start | bytes 131072 | tf_op jit(solution)/shard_map/slice | solution.py:11
  470.0 0.7 copy-start.4
  470.0 0.7 copy-start.5
  470.0 0.8 copy-start.6
  470.0 9.6 copy-start.3
  473.5 15.9 %all-to-all-start.1 = ((s32[128,2,2]{1,2,0:T(2,128)}), s32[128,2,2]{1,2,0:T(2,128)S(1)}, u32[]{:S(2)}, u32[]{:S(2)}) async-start(s32[128,2,2]{1,2,0:T(2,128)} %copy.18), calls=%async_computation.2 | async-start | bytes 262144 | tf_op jit(solution)/shard_map/all_to_all | solution.py:98
  489.4 14.3 %all-to-all-start = ((bf16[128,2,256]{2,1,0:T(2,128)(2,1)}), bf16[128,2,256]{2,1,0:T(2,128)(2,1)S(1)}, u32[]{:S(2)}, u32[]{:S(2)}) async-start(bf16[128,2,256]{2,1,0:T(2,128)(2,1)} %reshape.64), calls=%async_computation.1 | async-start | bytes 262144 | tf_op jit(solution)/shard_map/all_to_all | solution.py:91
  503.8 2.8 copy-start.1
  512.2 1.3 copy-start.2
  515.1 16.4 %all-to-all-start.2 = ((f32[128,2,256]{2,1,0:T(2,128)}), f32[128,2,256]{2,1,0:T(2,128)S(1)}, u32[]{:S(2)}, u32[]{:S(2)}) async-start(f32[128,2,256]{2,1,0:T(2,128)} %reshape.68), calls=%async_computation.3 | async-start | bytes 524288 | tf_op jit(solution)/shard_map/all_to_all | solution.py:113
Sparse Core Ops, SparseCore 0:
  11.0 72.5 all-gather.5
  109.3 67.6 all-gather.9
  180.5 67.6 all-gather.7
  470.2 663.5 reduce-scatter.1
where the time goes:
time: 1150 us; the launch traced here: 1140 us
  waiting for transfers between devices  791 us (69%)
  local copies, waits for them, and re-layouts  206 us (18%)
  matrix products  87.5 us (8%)
  other arithmetic  24.2 us (2%)
  starting transfers between devices  15.6 us (1%)
  between operations  14 us (1%)
    reduce_scatter x1, waiting for transfers between devices, per_device(): lax.psum_scatter(result, ('group', 'table'), scatter_dimension=0, tiled=T...  569 us
    dynamic_slice x127, local copies, waits for them, and re-layouts, hop(): return combine(so_far, jax.tree.map(lambda part: part[k], everything))  165 us
    all_gather x2, waiting for transfers between devices, merged(): everything = jax.tree.map(lambda part: lax.all_gather(part, axis), x)  125 us
    all_gather x1, waiting for transfers between devices, per_device(): gathered = lax.all_gather(user_vec, ('group', 'table'), axis=0, tiled=True)  75.6 us
    dot_general x8, matrix products, one_block(): return jnp.dot(probs_bf, cluster_rows, preferred_element_type=jnp.float32)  31.6 us
    dot_general x8, matrix products, add_cluster(): lax.dot_general(probs_bf, user_block, (((0,), (0,)), ((), ())), preferred...  30.5 us
    unnamed x18, local copies, waits for them, and re-layouts  29.4 us
  transfers between devices with their start and end apart: 7, of which 7 were waited for; matrix products, arithmetic and copies ran while one was open for 6% of the time, Pallas kernels for 0%

commit v1 on v0

v1 whole, which is shorter than its diff:
```python
import jax
import jax.numpy as jnp
from jax import lax
from jax.experimental import pallas as pl
from jax.experimental.pallas import tpu as pltpu
from jax.sharding import Mesh
from jax.sharding import PartitionSpec as P

BF = jnp.bfloat16
F32 = jnp.float32
LOG2E = 1.4426950408889634
ALL = ("y", "x", "z", "c")
PLANE = ("x", "z")
NT = (((1,), (1,)), ((), ()))
TN = (((0,), (0,)), ((), ()))
META = 128
VMEM = 56 << 20


def params():
    return pltpu.CompilerParams(vmem_limit_bytes=VMEM)


def whole(shape):
    return pl.BlockSpec(shape, lambda *ids: (0,) * len(shape))


def slot_pick(owner_row, slots):
    users = owner_row.shape[1]
    rows = lax.broadcasted_iota(jnp.int32, (users, users), 0)
    cols = lax.broadcasted_iota(jnp.int32, (users, users), 1)
    across = jnp.broadcast_to(owner_row, (users, users))
    down = jnp.sum(jnp.where(rows == cols, across, 0), axis=1, keepdims=True)
    earlier = (across == down) & (rows < cols)
    rank = jnp.sum(earlier.astype(jnp.int32), axis=0, keepdims=True)
    position = owner_row * 2 + rank
    return lax.broadcasted_iota(jnp.int32, (slots, users), 0) == position


def pack_kernel(user_ref, owner_ref, slot_ref, leaf_ref, out_ref):
    slots, width = out_ref.shape[0], user_ref.shape[1]
    users = user_ref.shape[0]
    pick = slot_pick(owner_ref[...], slots).astype(F32).astype(BF)
    out_ref[:, :width] = jnp.dot(pick, user_ref[...], preferred_element_type=F32).astype(BF)
    line = lax.broadcasted_iota(jnp.int32, (META, users), 0)
    leaf = leaf_ref[...]
    meta = jnp.where(line == 0, slot_ref[...] + 1, 0)
    meta = jnp.where(line == 1, leaf >> 6, meta)
    meta = jnp.where(line == 2, leaf & 63, meta)
    meta = meta.astype(F32).astype(BF)
    out_ref[:, width:] = lax.dot_general(pick, meta, NT, preferred_element_type=F32).astype(BF)


def pack(user_vec, owner, slot, leaf, slots):
    users, width = user_vec.shape
    return pl.pallas_call(
        pack_kernel,
        out_shape=jax.ShapeDtypeStruct((slots, width + META), BF),
        name="pack",
    )(user_vec, owner[None], slot[None], leaf[None])


def leaf_kernel(touched_ref, recv_ref, table_ref, cluster_ref, part_ref, grad_ref, label_ref, score_ref):
    k = pl.program_id(0)
    slots, width = part_ref.shape
    leaves = table_ref.shape[1]
    step = 512
    users = recv_ref[:, :width]
    meta = recv_ref[:, width:].astype(F32).T
    slot = meta[0:1, :] - 1.0
    leaf = (meta[1:2, :] * 64.0 + meta[2:3, :]).astype(jnp.int32)
    chosen = slot == k.astype(F32)
    leaf = jnp.where(chosen, leaf, -1)

    @pl.when(k == 0)
    def _():
        line = lax.broadcasted_iota(jnp.int32, (16, slots), 0)
        mine = (jnp.broadcast_to(slot, (16, slots)) == line.astype(F32)).astype(F32).astype(BF)
        label_ref[...] = jnp.dot(mine, users, preferred_element_type=F32)
        clusters = cluster_ref.shape[0]
        line = lax.broadcasted_iota(jnp.int32, (16, clusters), 0)
        column = lax.broadcasted_iota(jnp.int32, (16, clusters), 1)
        target = jnp.where(line == 0, touched_ref[0], jnp.where(line == 1, touched_ref[1], -1))
        pick = (column == target).astype(F32).astype(BF)
        rows = jnp.dot(pick, cluster_ref[...], preferred_element_type=F32).astype(BF)
        part_ref[...] = -lax.dot_general(mine, rows, TN, preferred_element_type=F32)

    peak = None
    for j in range(leaves // step):
        score = lax.dot_general(
            table_ref[0, pl.ds(j * step, step), :], users, NT, preferred_element_type=F32
        )
        score_ref[pl.ds(j * step, step), :] = score
        high = jnp.max(score.reshape(step // 8, 8, slots), axis=0)
        peak = high if peak is None else jnp.maximum(peak, high)
    peak = jnp.max(peak, axis=0, keepdims=True) * LOG2E
    total = jnp.zeros((8, slots), F32)
    for j in range(leaves // step):
        weight = jnp.exp2(score_ref[pl.ds(j * step, step), :] * LOG2E - peak)
        score_ref[pl.ds(j * step, step), :] = weight
        total = total + jnp.sum(weight.reshape(step // 8, 8, slots), axis=0)
    scale = chosen.astype(F32) / jnp.sum(total, axis=0, keepdims=True)
    part = jnp.zeros((slots, width), F32)
    for j in range(leaves // step):
        ids = lax.broadcasted_iota(jnp.int32, (step, slots), 0) + j * step
        coef = score_ref[pl.ds(j * step, step), :] * scale - (ids == leaf).astype(F32)
        coef = coef.astype(BF)
        grad_ref[0, pl.ds(j * step, step), :] = jnp.dot(
            coef, users, preferred_element_type=F32
        ).astype(BF)
        part = part + lax.dot_general(
            coef, table_ref[0, pl.ds(j * step, step), :], TN, preferred_element_type=F32
        )
    part_ref[...] += part


def leaf_pass(touched, recv, leaf_rows, cluster_rows):
    tables, leaves, width = leaf_rows.shape
    slots = recv.shape[0]
    return pl.pallas_call(
        leaf_kernel,
        grid=(tables,),
        in_specs=[
            pl.BlockSpec(memory_space=pltpu.SMEM),
            whole(recv.shape),
            pl.BlockSpec((1, leaves, width), lambda k: (k, 0, 0)),
            whole(cluster_rows.shape),
        ],
        out_specs=[
            whole((slots, width)),
            pl.BlockSpec((1, leaves, width), lambda k: (k, 0, 0)),
            whole((16, width)),
        ],
        out_shape=[
            jax.ShapeDtypeStruct((slots, width), F32),
            jax.ShapeDtypeStruct(leaf_rows.shape, BF),
            jax.ShapeDtypeStruct((16, width), F32),
        ],
        scratch_shapes=[pltpu.VMEM((leaves, slots), F32)],
        compiler_params=params(),
        name="leaf",
    )(touched, recv, leaf_rows, cluster_rows)


def score_kernel(*refs):
    parts = refs[:8]
    user_ref, exp_ref, acc_ref, stat_ref, score_ref, flip_ref = refs[8:]
    step = parts[0].shape[0]
    block, width = user_ref.shape

    @pl.when(pl.program_id(0) == 0)
    def _():
        for j, part in enumerate(parts):
            flip_ref[:, pl.ds(j * step, step)] = part[...].T

    users = user_ref[...]
    peak = None
    for j, part in enumerate(parts):
        score = lax.dot_general(part[...], users, NT, preferred_element_type=F32)
        score_ref[pl.ds(j * step, step), :] = score
        high = jnp.max(score.reshape(step // 8, 8, block), axis=0)
        peak = high if peak is None else jnp.maximum(peak, high)
    peak = jnp.max(peak, axis=0, keepdims=True)
    scaled = peak * LOG2E
    total = jnp.zeros((8, block), F32)
    acc = jnp.zeros((width, block), F32)
    for j in range(len(parts)):
        weight = jnp.exp2(score_ref[pl.ds(j * step, step), :] * LOG2E - scaled)
        total = total + jnp.sum(weight.reshape(step // 8, 8, block), axis=0)
        weight = weight.astype(BF)
        exp_ref[pl.ds(j * step, step), :] = weight
        acc = acc + jnp.dot(
            flip_ref[:, pl.ds(j * step, step)], weight, preferred_element_type=F32
        )
    acc_ref[...] = acc.T.astype(BF)
    stat_ref[0:1, :] = peak
    stat_ref[1:2, :] = jnp.sum(total, axis=0, keepdims=True)


def score_pass(parts, users):
    step, width = parts[0].shape
    clusters = step * len(parts)
    count = users.shape[0]
    block = 512
    return pl.pallas_call(
        score_kernel,
        grid=(count // block,),
        in_specs=[whole((step, width))] * len(parts)
        + [pl.BlockSpec((block, width), lambda i: (i, 0))],
        out_specs=[
            pl.BlockSpec((clusters, block), lambda i: (0, i)),
            pl.BlockSpec((block, width), lambda i: (i, 0)),
            pl.BlockSpec((2, block), lambda i: (0, i)),
        ],
        out_shape=[
            jax.ShapeDtypeStruct((clusters, count), BF),
            jax.ShapeDtypeStruct((count, width), BF),
            jax.ShapeDtypeStruct((2, count), F32),
        ],
        scratch_shapes=[
            pltpu.VMEM((clusters, block), F32),
            pltpu.VMEM((width, clusters), BF),
        ],
        compiler_params=params(),
        name="scores",
    )(*parts, users)


def merge_stats(stats):
    peak = jnp.max(stats[:, 0, :], axis=0, keepdims=True)
    total = jnp.sum(stats[:, 1, :] * jnp.exp(stats[:, 0, :] - peak), axis=0, keepdims=True)
    return peak, total


def scale_kernel(stats_ref, mine_ref, user_ref, out_ref):
    peak, total = merge_stats(stats_ref[...])
    weight = jnp.exp(mine_ref[0:1, :] - peak) / total
    weight = jnp.broadcast_to(weight, (128, weight.shape[1])).T
    out_ref[...] = (user_ref[...].astype(F32) * weight[:, 0:1]).astype(BF)


def scale_users(stats, mine, users):
    return pl.pallas_call(
        scale_kernel,
        out_shape=jax.ShapeDtypeStruct(users.shape, BF),
        compiler_params=params(),
        name="scale_users",
    )(stats, mine, users)


def cluster_kernel(exp_ref, user_ref, out_ref):
    out_ref[...] = jnp.dot(exp_ref[...], user_ref[...], preferred_element_type=F32)


def cluster_pass(weights, users, half):
    clusters, count = weights.shape
    width = users.shape[1]
    block = 1024
    steps = clusters // 2 // block
    return pl.pallas_call(
        cluster_kernel,
        grid=(steps,),
        in_specs=[
            pl.BlockSpec((block, count), lambda i: (i + half * steps, 0)),
            whole((count, width)),
        ],
        out_specs=pl.BlockSpec((block, width), lambda i: (i, 0)),
        out_shape=jax.ShapeDtypeStruct((clusters // 2, width), F32),
        compiler_params=params(),
        name="cluster_sums",
    )(weights, users)


def home_kernel(acc_ref, stats_ref, owner_ref, back_ref, out_ref):
    peers, users, width = acc_ref.shape
    stats = stats_ref[...]
    peak, total = merge_stats(stats)
    factor = jnp.exp(stats[:, 0, :] - peak) / total
    factor = factor.T
    slots = back_ref.shape[0]
    pick = slot_pick(owner_ref[...], slots).astype(F32)
    out = lax.dot_general(
        pick, back_ref[...], TN, preferred_element_type=F32, precision=lax.Precision.HIGHEST
    )
    for q in range(peers):
        out = out + acc_ref[q].astype(F32) * factor[:, q : q + 1]
    out_ref[...] = out


def home_pass(acc, stats, owner, back):
    return pl.pallas_call(
        home_kernel,
        out_shape=jax.ShapeDtypeStruct(acc.shape[1:], F32),
        compiler_params=params(),
        name="home",
    )(acc, stats, owner[None], back)


def shift(x, axis, by):
    size = lax.axis_size(axis)
    return lax.ppermute(x, axis, [(i, (i + by) % size) for i in range(size)])


def swap(x, axis):
    return lax.all_to_all(x, axis, 0, 0, tiled=True)


def per_device(user_vec, cluster_rows, leaf_rows, touched, route_owner, route_slot, leaf_label):
    owners = lax.axis_size(ALL)
    rows = lax.axis_size("y")
    peers = lax.axis_size(PLANE)
    count, width = user_vec.shape
    slots = 2 * owners

    users = swap(jnp.broadcast_to(user_vec[None], (peers, count, width)), PLANE)
    users = users.reshape(peers * count, width)
    near = [cluster_rows] + [shift(cluster_rows, "y", -j) for j in range(1, rows)]
    far = [shift(part, "c", 1) for part in near]

    sent = pack(user_vec, route_owner, route_slot, leaf_label, slots)
    recv = swap(sent.reshape(owners, 2, width + META), ALL).reshape(slots, width + META)

    weights, acc, mine = score_pass(near + far, users)
    stats = swap(jnp.broadcast_to(mine[None], (peers,) + mine.shape), PLANE)
    acc = swap(acc.reshape(peers, count, width), PLANE)

    leaf_part, leaf_grad, labels = leaf_pass(touched, recv, leaf_rows, cluster_rows)
    back = swap(leaf_part.reshape(owners, 2, width), ALL).reshape(slots, width)

    scaled = scale_users(stats, mine, users)
    other = shift(cluster_pass(weights, scaled, 1), "c", 1)
    both = (cluster_pass(weights, scaled, 0) + other).reshape(rows, -1, width)
    cluster_grad = both[0]
    for j in range(1, rows):
        cluster_grad = cluster_grad + shift(both[j].astype(BF), "y", j).astype(F32)
    ids = jnp.arange(cluster_rows.shape[0])[:, None]
    for k in range(2):
        cluster_grad = cluster_grad - jnp.where(ids == touched[k], labels[k][None], 0.0)

    place = lax.axis_index(PLANE)
    stats_home = lax.dynamic_slice_in_dim(stats, place * count, count, 2)
    user_grad = home_pass(acc, stats_home, route_owner, back)
    return user_grad, cluster_grad, leaf_grad


def solution(mesh):
    grid = Mesh(mesh.devices.reshape(4, 4, 4, 2), ALL)
    one = P(ALL)
    return jax.shard_map(
        per_device,
        mesh=grid,
        in_specs=(P(ALL, None), P(ALL, None), P(ALL, None, None), one, one, one, one),
        out_specs=(P(ALL, None), P(ALL, None), P(ALL, None, None)),
        check_vma=False,
    )
```

time: 1150 us -> 151 us (0.13)
  waiting for transfers between devices: 791 us -> 23.6 us
  local copies, waits for them, and re-layouts: 206 us -> 12 us
  matrix products: 87.5 us -> 0 us
  Pallas kernels: 0 us -> 50 us
  blocking collectives: 0 us -> 30.2 us
  other arithmetic: 24.2 us -> 6.56 us
  between operations: 14 us -> 0.83 us
    reduce_scatter x1 -> x0, waiting for transfers between devices: 569 us -> none  [per_device(): lax.psum_scatter(result, ('group', 'table'), scatter_dimension=0, tiled=T...]
    all_gather x3 -> x0, waiting for transfers between devices: 201 us -> none  [the longest x2 125 us: merged(): everything = jax.tree.map(lambda part: lax.all_gather(part, axis), x)]
    dynamic_slice x143 -> x1, local copies, waits for them, and re-layouts: 165 us -> 1.32 us  [per_device(): stats_home = lax.dynamic_slice_in_dim(stats, place * count, count, 2)]
    dot_general x31 -> x0, matrix products: 87.5 us -> none  [the longest x8 31.6 us: one_block(): return jnp.dot(probs_bf, cluster_rows, preferred_element_type=jnp.float32)]
    pallas_call x0 -> x7, Pallas kernels: none -> 50 us  [the longest x1 20.7 us: score_pass(): pl.pallas_call(score_kernel, grid=(count // block,), in_specs=[whole((ste...]
    all_to_all x0 -> x2, blocking collectives: none -> 30.2 us  [swap(): return lax.all_to_all(x, axis, 0, 0, tiled=True)]
    unnamed x18 -> x24, local copies, waits for them, and re-layouts: 29.4 us -> 2.02 us
    ppermute x0 -> x11, waiting for transfers between devices: none -> 14 us  [shift(): return lax.ppermute(x, axis, [(i, (i + by) % size) for i in range(size)])]
  transfers between devices with their start and end apart: 7 -> 14, of which waited for: 7 -> 5; matrix products, arithmetic and copies ran while one was open for 6% -> 8% of each run, Pallas kernels for 0% -> 13%
where the time goes in v1:
time: 151 us; the launch traced here: 150 us
  Pallas kernels  50 us (33%)
  blocking collectives  30.2 us (20%)
  starting transfers between devices  26.8 us (18%)
  waiting for transfers between devices  23.6 us (16%)
  local copies, waits for them, and re-layouts  12 us (8%)
  other arithmetic  6.56 us (4%)
    all_to_all x2, blocking collectives, swap(): return lax.all_to_all(x, axis, 0, 0, tiled=True)  30.2 us
    pallas_call x1, Pallas kernels, score_pass(): pl.pallas_call(score_kernel, grid=(count // block,), in_specs=[whole((ste...  20.7 us
    all_to_all x3, starting transfers between devices, swap(): return lax.all_to_all(x, axis, 0, 0, tiled=True)  16.4 us
    ppermute x11, waiting for transfers between devices, shift(): return lax.ppermute(x, axis, [(i, (i + by) % size) for i in range(size)])  14 us
    pallas_call x2, Pallas kernels, cluster_pass(): pl.pallas_call(cluster_kernel, grid=(steps,), in_specs=[pl.BlockSpec((blo...  12 us
    ppermute x11, starting transfers between devices, shift(): return lax.ppermute(x, axis, [(i, (i + by) % size) for i in range(size)])  10.4 us
    pallas_call x1, Pallas kernels, leaf_pass(): pl.pallas_call(leaf_kernel, grid=(tables,), in_specs=[pl.BlockSpec(memory...  9.67 us
    all_to_all x3, waiting for transfers between devices, swap(): return lax.all_to_all(x, axis, 0, 0, tiled=True)  9.61 us
  transfers between devices with their start and end apart: 14, of which 5 were waited for; matrix products, arithmetic and copies ran while one was open for 8% of the time, Pallas kernels for 13%

profile of v1, /device:TPU:0, one launch (start us, length us, event | category | flops | bytes accessed | tf_op | source)
XLA Modules:
  0.0 149.9 jit_solution(13074705068078851868)
XLA Ops:
  0.6 0.0 copy-start.3
  0.6 2.0 %broadcast_in_dim.58 = bf16[16,128,256]{2,1,0:T(8,128)(2,1)} broadcast(bf16[128,256]{1,0:T(8,128)(2,1)} %user_ref.1), dimensions={1,2} | broadcast | bytes 1114112 | tf_op jit(solution)/shard_map/broadcast_in_dim | solution.py:295
  2.6 8.0 %all-to-all-start = ((bf16[16,128,256]{2,1,0:T(8,128)(2,1)}), bf16[16,128,256]{2,1,0:T(8,128)(2,1)S(1)}, u32[]{:S(2)}, u32[]{:S(2)}) async-start(bf16[16,128,256]{2,1,0:T(8,128)(2,1)} %broadcast_in_dim.58), calls=%async_computation | async-start | bytes 2097152 | tf_op jit(solution)/shard_map/all_to_all | solution.py:285
  10.6 3.1 %collective-permute-start = (bf16[512,256]{1,0:T(8,128)(2,1)S(1)}, bf16[512,256]{1,0:T(8,128)(2,1)S(1)}, u32[]{:S(2)}, u32[]{:S(2)}) collective-permute-start(bf16[512,256]{1,0:T(8,128)(2,1)S(1)} %copy-done.3), channel_id=1, source_target_pairs={{0,96},{32,0},{64,32},{96,64},{1,97},{33,1},{65,33},{97,65},{2,98}... | collective-permute-start | bytes 786440 | tf_op jit(solution)/shard_map/ppermute | solution.py:281
  13.7 0.6 collective-permute-start.1
  14.3 1.0 collective-permute-start.2
  15.3 0.0 collective-permute-start.3
  15.3 9.3 %collective-permute-done.refs_1_ = bf16[512,256]{1,0:T(8,128)(2,1)S(1)} collective-permute-done((bf16[512,256]{1,0:T(8,128)(2,1)S(1)}, bf16[512,256]{1,0:T(8,128)(2,1)S(1)}, u32[]{:S(2)}, u32[]{:S(2)}) %collective-permute-start) | collective-permute-done | bytes 262176 | tf_op jit(solution)/shard_map/ppermute | solution.py:281
  24.6 0.0 collective-permute-start.4
  24.6 0.0 collective-permute-done.1.refs_2_
  24.6 0.5 collective-permute-start.5
  25.1 3.2 %collective-permute-done.2.refs_3_ = bf16[512,256]{1,0:T(8,128)(2,1)S(1)} collective-permute-done((bf16[512,256]{1,0:T(8,128)(2,1)S(1)}, bf16[512,256]{1,0:T(8,128)(2,1)S(1)}, u32[]{:S(2)}, u32[]{:S(2)}) %collective-permute-start.2) | collective-permute-done | bytes 262176 | tf_op jit(solution)/shard_map/ppermute | solution.py:281
  28.3 0.0 collective-permute-start.6
  28.3 0.0 collective-permute-done.5.refs_6_
  28.3 1.5 collective-permute-done.6.refs_7_
  29.9 0.6 copy-done.10
  30.5 0.3 copy-done
  30.9 20.7 %scores.1 = (bf16[4096,2048]{1,0:T(8,128)(2,1)}, bf16[2048,256]{1,0:T(8,128)(2,1)}, f32[2,2048]{1,0:T(2,128)}) custom-call(bf16[512,256]{1,0:T(8,128)(2,1)} %cluster_ref.1, bf16[512,256]{1,0:T(8,128)(2,1)} %copy-done.4, bf16[512,256]{1,0:T(8,128)(2,1)} %copy-done.5, bf16[512,256]{1,0:T(8,128)(2,1)} %copy-done.6, bf16[512,256]{1,0:T(8,128)(2,1)} %copy-done.7, ...), custom_call_target="tpu_custom_call" | custom-call | tf_op jit(solution)/shard_map/scores/pallas_call | solution.py:185
  51.5 0.8 broadcast_in_dim.59
  52.3 15.6 %all_to_all.25.stats_ref = f32[16,2,2048]{2,1,0:T(2,128)} all-to-all(f32[16,2,2048]{2,1,0:T(2,128)S(1)} %broadcast_in_dim.59), channel_id=1, replica_groups=mesh['y'=4,'x'=4,'z'=4,'c'=2] {'x','z'}, dimensions={0} | all-to-all | bytes 524288 | tf_op jit(solution)/shard_map/all_to_all | solution.py:285
  68.0 3.1 %scale_users.1.user_ref = bf16[2048,256]{1,0:T(8,128)(2,1)} custom-call(f32[16,2,2048]{2,1,0:T(2,128)} %all_to_all.25.stats_ref, f32[2,2048]{1,0:T(2,128)} %get-tuple-element.10.mine_ref, bf16[2048,256]{1,0:T(8,128)(2,1)} %bitcast.10), custom_call_target="tpu_custom_call" | custom-call | tf_op jit(solution)/shard_map/scale_users/pallas_call | solution.py:223
  71.1 6.0 %cluster_sums.3 = f32[2048,256]{1,0:T(8,128)} custom-call(bf16[4096,2048]{1,0:T(8,128)(2,1)} %get-tuple-element.12.exp_ref, bf16[2048,256]{1,0:T(8,128)(2,1)} %scale_users.1.user_ref), custom_call_target="tpu_custom_call" | custom-call | tf_op jit(solution)/shard_map/cluster_sums/pallas_call | solution.py:240
  77.1 0.0 collective-permute-start.7
  77.1 1.8 %pack.1 = bf16[256,384]{1,0:T(8,128)(2,1)} custom-call(bf16[128,256]{1,0:T(8,128)(2,1)} %user_ref.1, s32[1,128]{1,0:T(1,128)} %bitcast.14, s32[1,128]{1,0:T(1,128)} %bitcast.16, s32[1,128]{1,0:T(1,128)} %bitcast.17), custom_call_target="tpu_custom_call" | custom-call | tf_op jit(solution)/shard_map/pack/pallas_call | solution.py:56
  78.9 1.0 reshape.47
  79.9 14.5 %all_to_all.26 = bf16[128,2,384]{2,1,0:T(2,128)(2,1)S(1)} all-to-all(bf16[128,2,384]{2,1,0:T(2,128)(2,1)S(1)} %reshape.47), channel_id=1, replica_groups=mesh['y'=4,'x'=4,'z'=4,'c'=2] {'y','x','z','c'}, dimensions={0} | all-to-all | bytes 393216 | tf_op jit(solution)/shard_map/all_to_all | solution.py:285
  94.5 0.7 reshape.48.recv_ref
  95.2 9.7 %leaf.1 = (f32[256,256]{1,0:T(8,128)}, bf16[2,4096,256]{2,1,0:T(8,128)(2,1)}, f32[16,256]{1,0:T(8,128)}) custom-call(s32[2]{0:T(128)} %touched_ref.1, bf16[256,384]{1,0:T(8,128)(2,1)} %reshape.48.recv_ref, bf16[2,4096,256]{2,1,0:T(8,128)(2,1)} %table_ref.1, bf16[512,256]{1,0:T(8,128)(2,1)} %cluster_ref.1), custom_call_target="tpu_custom_call" | custom-call | tf_op jit(solution)/shard_map/leaf/pallas_call | solution.py:120
  104.9 1.8 %reshape.49 = f32[128,2,256]{2,1,0:T(2,128)} reshape(f32[256,256]{1,0:T(8,128)} %get-tuple-element.11) | data formatting | bytes 524288 | tf_op jit(solution)/shard_map/reshape | solution.py:308
  106.7 4.6 %all-to-all-start.4 = ((f32[128,2,256]{2,1,0:T(2,128)}), f32[128,2,256]{2,1,0:T(2,128)S(1)}, u32[]{:S(2)}, u32[]{:S(2)}) async-start(f32[128,2,256]{2,1,0:T(2,128)} %reshape.49), calls=%async_computation.4 | async-start | bytes 524288 | tf_op jit(solution)/shard_map/all_to_all | solution.py:285
  111.4 0.6 fusion.7
  112.0 1.3 iota_compare_fusion
  113.2 6.0 %cluster_sums.2 = f32[2048,256]{1,0:T(8,128)} custom-call(bf16[4096,2048]{1,0:T(8,128)(2,1)} %get-tuple-element.12.exp_ref, bf16[2048,256]{1,0:T(8,128)(2,1)} %scale_users.1.user_ref), custom_call_target="tpu_custom_call" | custom-call | tf_op jit(solution)/shard_map/cluster_sums/pallas_call | solution.py:240
  119.3 3.0 %all-to-all-done.4 = f32[128,2,256]{2,1,0:T(2,128)S(1)} async-done(((f32[128,2,256]{2,1,0:T(2,128)}), f32[128,2,256]{2,1,0:T(2,128)S(1)}, u32[]{:S(2)}, u32[]{:S(2)}) %all-to-all-start.4) | async-done | bytes 262176 | tf_op jit(solution)/shard_map/all_to_all | solution.py:285
  122.2 3.8 %all-to-all-start.1 = ((bf16[16,128,256]{2,1,0:T(8,128)(2,1)}), bf16[16,128,256]{2,1,0:T(8,128)(2,1)S(1)}, u32[]{:S(2)}, u32[]{:S(2)}) async-start(bf16[16,128,256]{2,1,0:T(8,128)(2,1)} %bitcast.11), calls=%async_computation.1 | async-start | bytes 2097152 | tf_op jit(solution)/shard_map/all_to_all | solution.py:285
  126.1 0.0 collective-permute-done.7
  126.1 3.2 %fusion.4 = (bf16[2048,256]{1,0:T(8,128)(2,1)S(1)}, f32[2048,256]{1,0:T(8,128)}) fusion(f32[2048,256]{1,0:T(8,128)S(1)} %copy-done.1, f32[2048,256]{1,0:T(8,128)} %collective-permute-done.7), kind=kLoop, calls=%fused_computation.8 | loop fusion | flops 1048576 | bytes 7340032 | tf_op jit(solution)/shard_map/convert.2
  129.3 0.1 fusion.5
  129.4 2.9 %collective-permute-start.10 = (bf16[512,256]{1,0:T(8,128)(2,1)S(1)}, bf16[512,256]{1,0:T(8,128)(2,1)S(1)}, u32[]{:S(2)}, u32[]{:S(2)}) collective-permute-start(bf16[512,256]{1,0:T(8,128)(2,1)S(1)} %get-tuple-element.18), channel_id=1, source_target_pairs={{0,96},{32,0},{64,32},{96,64},{1,97},{33,1},{65,33},{97,65},{2,98}... | collective-permute-start | bytes 786440 | tf_op jit(solution)/shard_map/ppermute | solution.py:281
  132.4 0.0 collective-permute-start.8
  132.4 2.2 %collective-permute-start.9 = (bf16[512,256]{1,0:T(8,128)(2,1)S(1)}, bf16[512,256]{1,0:T(8,128)(2,1)S(1)}, u32[]{:S(2)}, u32[]{:S(2)}) collective-permute-start(bf16[512,256]{1,0:T(8,128)(2,1)S(1)} %get-tuple-element.19), channel_id=1, source_target_pairs={{0,64},{32,96},{64,0},{96,32},{1,65},{33,97},{65,1},{97,33},{2,66}... | collective-permute-start | bytes 786440 | tf_op jit(solution)/shard_map/ppermute | solution.py:281
  134.6 0.8 fusion.6
  135.4 0.9 reshape.50.back_ref
  136.3 1.3 constant_dynamic-slice_fusion.stats_ref
  137.6 6.6 %all-to-all-done.1.acc_ref = bf16[16,128,256]{2,1,0:T(8,128)(2,1)S(1)} async-done(((bf16[16,128,256]{2,1,0:T(8,128)(2,1)}), bf16[16,128,256]{2,1,0:T(8,128)(2,1)S(1)}, u32[]{:S(2)}, u32[]{:S(2)}) %all-to-all-start.1) | async-done | bytes 1048608 | tf_op jit(solution)/shard_map/all_to_all | solution.py:285
  144.2 1.0 copy-done.2
  145.2 2.7 %home.1 = f32[128,256]{1,0:T(8,128)} custom-call(bf16[16,128,256]{2,1,0:T(8,128)(2,1)} %copy-done.2, f32[16,2,128]{2,1,0:T(2,128)} %constant_dynamic-slice_fusion.stats_ref, s32[1,128]{1,0:T(1,128)} %bitcast.15, f32[256,256]{1,0:T(8,128)} %reshape.50.back_ref), custom_call_target="tpu_custom_call" | custom-call | tf_op jit(solution)/shard_map/home/pallas_call | solution.py:271
  147.9 2.0 %fusion.3 = f32[512,256]{1,0:T(8,128)} fusion(f32[2048,256]{1,0:T(8,128)} %get-tuple-element.16, bf16[512,256]{1,0:T(8,128)(2,1)S(1)} %collective-permute-done.10, bf16[512,256]{1,0:T(8,128)(2,1)S(1)} %collective-permute-done.9, bf16[512,256]{1,0:T(8,128)(2,1)S(1)} %collective-permute-done.8, f32[256]{0:T(256)S(1)} %bitcast.13, f32[256]{0:T(256)S(1)} %bitcast.12, ...), kind=kLoop, calls=%fused_computation.4 | loop fusion | flops 1310720 | bytes 1838080 | tf_op jit(solution)/shard_map/sub | solution.py:318
  (26 shorter events, 0.1 us)
Async XLA Ops:
  0.6 9.9 %copy-start.3 = (bf16[512,256]{1,0:T(8,128)(2,1)S(1)}, bf16[512,256]{1,0:T(8,128)(2,1)}, u32[]{:S(2)}) copy-start(bf16[512,256]{1,0:T(8,128)(2,1)} %cluster_ref.1) | copy-start | bytes 786436
  2.6 27.2 %all-to-all-start = ((bf16[16,128,256]{2,1,0:T(8,128)(2,1)}), bf16[16,128,256]{2,1,0:T(8,128)(2,1)S(1)}, u32[]{:S(2)}, u32[]{:S(2)}) async-start(bf16[16,128,256]{2,1,0:T(8,128)(2,1)} %broadcast_in_dim.58), calls=%async_computation | async-start | bytes 2097152 | tf_op jit(solution)/shard_map/all_to_all | solution.py:285
  10.6 14.0 %collective-permute-start = (bf16[512,256]{1,0:T(8,128)(2,1)S(1)}, bf16[512,256]{1,0:T(8,128)(2,1)S(1)}, u32[]{:S(2)}, u32[]{:S(2)}) collective-permute-start(bf16[512,256]{1,0:T(8,128)(2,1)S(1)} %copy-done.3), channel_id=1, source_target_pairs={{0,96},{32,0},{64,32},{96,64},{1,97},{33,1},{65,33},{97,65},{2,98}... | collective-permute-start | bytes 786440 | tf_op jit(solution)/shard_map/ppermute | solution.py:281
  13.7 10.9 %collective-permute-start.1 = (bf16[512,256]{1,0:T(8,128)(2,1)S(1)}, bf16[512,256]{1,0:T(8,128)(2,1)S(1)}, u32[]{:S(2)}, u32[]{:S(2)}) collective-permute-start(bf16[512,256]{1,0:T(8,128)(2,1)S(1)} %copy-done.3), channel_id=1, source_target_pairs={{0,64},{32,96},{64,0},{96,32},{1,65},{33,97},{65,1},{97,33},{2,66}... | collective-permute-start | bytes 786440 | tf_op jit(solution)/shard_map/ppermute | solution.py:281
  14.3 14.0 %collective-permute-start.2 = (bf16[512,256]{1,0:T(8,128)(2,1)S(1)}, bf16[512,256]{1,0:T(8,128)(2,1)S(1)}, u32[]{:S(2)}, u32[]{:S(2)}) collective-permute-start(bf16[512,256]{1,0:T(8,128)(2,1)S(1)} %copy-done.3), channel_id=1, source_target_pairs={{0,32},{32,64},{64,96},{96,0},{1,33},{33,65},{65,97},{97,1},{2,34}... | collective-permute-start | bytes 786440 | tf_op jit(solution)/shard_map/ppermute | solution.py:281
  15.3 13.0 %collective-permute-start.3 = (bf16[512,256]{1,0:T(8,128)(2,1)S(1)}, bf16[512,256]{1,0:T(8,128)(2,1)S(1)}, u32[]{:S(2)}, u32[]{:S(2)}) collective-permute-start(bf16[512,256]{1,0:T(8,128)(2,1)S(1)} %copy-done.3), channel_id=1, source_target_pairs={{0,1},{1,0},{2,3},{3,2},{4,5},{5,4},{6,7},{7,6},{8,9},{9,8},{10,11... | collective-permute-start | bytes 786440 | tf_op jit(solution)/shard_map/ppermute | solution.py:281
  24.6 5.3 %copy-start.4 = (bf16[512,256]{1,0:T(8,128)(2,1)}, bf16[512,256]{1,0:T(8,128)(2,1)S(1)}, u32[]{:S(2)}) copy-start(bf16[512,256]{1,0:T(8,128)(2,1)S(1)} %collective-permute-done.refs_1_) | copy-start | bytes 786436
  24.6 3.7 %collective-permute-start.4 = (bf16[512,256]{1,0:T(8,128)(2,1)S(1)}, bf16[512,256]{1,0:T(8,128)(2,1)S(1)}, u32[]{:S(2)}, u32[]{:S(2)}) collective-permute-start(bf16[512,256]{1,0:T(8,128)(2,1)S(1)} %collective-permute-done.refs_1_), channel_id=1, source_target_pairs={{0,1},{1,0},{2,3},{3,2},{4,5},{5,4},{6,7},{7,6},{8,9},{9,8},{10,11... | collective-permute-start | bytes 786440 | tf_op jit(solution)/shard_map/ppermute | solution.py:281
  24.6 5.3 %copy-start.5 = (bf16[512,256]{1,0:T(8,128)(2,1)}, bf16[512,256]{1,0:T(8,128)(2,1)S(1)}, u32[]{:S(2)}) copy-start(bf16[512,256]{1,0:T(8,128)(2,1)S(1)} %collective-permute-done.1.refs_2_) | copy-start | bytes 786436
  24.6 3.7 %collective-permute-start.5 = (bf16[512,256]{1,0:T(8,128)(2,1)S(1)}, bf16[512,256]{1,0:T(8,128)(2,1)S(1)}, u32[]{:S(2)}, u32[]{:S(2)}) collective-permute-start(bf16[512,256]{1,0:T(8,128)(2,1)S(1)} %collective-permute-done.1.refs_2_), channel_id=1, source_target_pairs={{0,1},{1,0},{2,3},{3,2},{4,5},{5,4},{6,7},{7,6},{8,9},{9,8},{10,11... | collective-permute-start | bytes 786440 | tf_op jit(solution)/shard_map/ppermute | solution.py:281
  28.3 1.6 %copy-start.6 = (bf16[512,256]{1,0:T(8,128)(2,1)}, bf16[512,256]{1,0:T(8,128)(2,1)S(1)}, u32[]{:S(2)}) copy-start(bf16[512,256]{1,0:T(8,128)(2,1)S(1)} %collective-permute-done.2.refs_3_) | copy-start | bytes 786436
  28.3 1.5 %collective-permute-start.6 = (bf16[512,256]{1,0:T(8,128)(2,1)S(1)}, bf16[512,256]{1,0:T(8,128)(2,1)S(1)}, u32[]{:S(2)}, u32[]{:S(2)}) collective-permute-start(bf16[512,256]{1,0:T(8,128)(2,1)S(1)} %collective-permute-done.2.refs_3_), channel_id=1, source_target_pairs={{0,1},{1,0},{2,3},{3,2},{4,5},{5,4},{6,7},{7,6},{8,9},{9,8},{10,11... | collective-permute-start | bytes 786440 | tf_op jit(solution)/shard_map/ppermute | solution.py:281
  28.3 1.6 %copy-start.7 = (bf16[512,256]{1,0:T(8,128)(2,1)}, bf16[512,256]{1,0:T(8,128)(2,1)S(1)}, u32[]{:S(2)}) copy-start(bf16[512,256]{1,0:T(8,128)(2,1)S(1)} %collective-permute-done.3.refs_4_) | copy-start | bytes 786436
  28.3 1.6 %copy-start.8 = (bf16[512,256]{1,0:T(8,128)(2,1)}, bf16[512,256]{1,0:T(8,128)(2,1)S(1)}, u32[]{:S(2)}) copy-start(bf16[512,256]{1,0:T(8,128)(2,1)S(1)} %collective-permute-done.4.refs_5_) | copy-start | bytes 786436
  28.3 1.5 %copy-start.9 = (bf16[512,256]{1,0:T(8,128)(2,1)}, bf16[512,256]{1,0:T(8,128)(2,1)S(1)}, u32[]{:S(2)}) copy-start(bf16[512,256]{1,0:T(8,128)(2,1)S(1)} %collective-permute-done.5.refs_6_) | copy-start | bytes 786436
  29.8 0.7 copy-start.10
  29.8 1.1 copy-start
  77.1 49.0 %collective-permute-start.7 = (f32[2048,256]{1,0:T(8,128)}, f32[2048,256]{1,0:T(8,128)}, u32[]{:S(2)}, u32[]{:S(2)}) collective-permute-start(f32[2048,256]{1,0:T(8,128)} %cluster_sums.3), channel_id=1, source_target_pairs={{0,1},{1,0},{2,3},{3,2},{4,5},{5,4},{6,7},{7,6},{8,9},{9,8},{10,11... | collective-permute-start | bytes 6291464 | tf_op jit(solution)/shard_map/ppermute | solution.py:281
  95.2 16.1 %copy-start.11 = (s32[2]{0:T(128)S(1)}, s32[2]{0:T(128)}, u32[]{:S(2)}) copy-start(s32[2]{0:T(128)} %touched_ref.1) | copy-start | bytes 28
  106.7 15.5 %all-to-all-start.4 = ((f32[128,2,256]{2,1,0:T(2,128)}), f32[128,2,256]{2,1,0:T(2,128)S(1)}, u32[]{:S(2)}, u32[]{:S(2)}) async-start(f32[128,2,256]{2,1,0:T(2,128)} %reshape.49), calls=%async_computation.4 | async-start | bytes 524288 | tf_op jit(solution)/shard_map/all_to_all | solution.py:285
  119.3 6.8 %copy-start.1 = (f32[2048,256]{1,0:T(8,128)S(1)}, f32[2048,256]{1,0:T(8,128)}, u32[]{:S(2)}) copy-start(f32[2048,256]{1,0:T(8,128)} %cluster_sums.2) | copy-start | bytes 6291460
  122.2 22.0 %all-to-all-start.1 = ((bf16[16,128,256]{2,1,0:T(8,128)(2,1)}), bf16[16,128,256]{2,1,0:T(8,128)(2,1)S(1)}, u32[]{:S(2)}, u32[]{:S(2)}) async-start(bf16[16,128,256]{2,1,0:T(8,128)(2,1)} %bitcast.11), calls=%async_computation.1 | async-start | bytes 2097152 | tf_op jit(solution)/shard_map/all_to_all | solution.py:285
  129.4 18.5 %collective-permute-start.10 = (bf16[512,256]{1,0:T(8,128)(2,1)S(1)}, bf16[512,256]{1,0:T(8,128)(2,1)S(1)}, u32[]{:S(2)}, u32[]{:S(2)}) collective-permute-start(bf16[512,256]{1,0:T(8,128)(2,1)S(1)} %get-tuple-element.18), channel_id=1, source_target_pairs={{0,96},{32,0},{64,32},{96,64},{1,97},{33,1},{65,33},{97,65},{2,98}... | collective-permute-start | bytes 786440 | tf_op jit(solution)/shard_map/ppermute | solution.py:281
  132.4 15.5 %collective-permute-start.8 = (bf16[512,256]{1,0:T(8,128)(2,1)S(1)}, bf16[512,256]{1,0:T(8,128)(2,1)S(1)}, u32[]{:S(2)}, u32[]{:S(2)}) collective-permute-start(bf16[512,256]{1,0:T(8,128)(2,1)S(1)} %get-tuple-element.17), channel_id=1, source_target_pairs={{0,32},{32,64},{64,96},{96,0},{1,33},{33,65},{65,97},{97,1},{2,34}... | collective-permute-start | bytes 786440 | tf_op jit(solution)/shard_map/ppermute | solution.py:281
  132.4 15.5 %collective-permute-start.9 = (bf16[512,256]{1,0:T(8,128)(2,1)S(1)}, bf16[512,256]{1,0:T(8,128)(2,1)S(1)}, u32[]{:S(2)}, u32[]{:S(2)}) collective-permute-start(bf16[512,256]{1,0:T(8,128)(2,1)S(1)} %get-tuple-element.19), channel_id=1, source_target_pairs={{0,64},{32,96},{64,0},{96,32},{1,65},{33,97},{65,1},{97,33},{2,66}... | collective-permute-start | bytes 786440 | tf_op jit(solution)/shard_map/ppermute | solution.py:281
  144.2 1.0 copy-start.2
